TPU v7x, 32 devices: a whole 2x2x4 slice. The times are simulated.
32 devices in a mesh: grp: 2 (over x), exp: 4 (over y, core), base: 4 (over z).
Axes of the slice: x: 2, y: 2, z: 4, core: 2. Of those that a mesh axis runs over, the one named last changes fastest.
Arguments:
- tokens: bfloat16 [512, 7168], P(('grp', 'exp'), 'base'), parts along dimension 0, may hold values from -6 to 6
- expert_ids: int32 [512, 8], P(('grp', 'exp')), parts along dimension 0, may hold values from 0 to 15, all different within a row; in each aligned block of 64 rows (0 to 63, 64 to 127, ...) at most 48 rows name the same one
- gate_q: int32 [512, 8], P(('grp', 'exp')), parts along dimension 0, may hold values from 1 to 65536
- importance: float32 [7168], P('base'), may hold values from 0.5 to 18
- dense_gate: bfloat16 [16, 7168, 1024], P('exp', None, 'base'), may hold values from -0.0625 to 0.0625
- dense_up: bfloat16 [16, 7168, 1024], P('exp', None, 'base'), may hold values from -0.0625 to 0.0625
- dense_down: bfloat16 [16, 1024, 7168], P('exp', None, 'base'), may hold values from -0.1875 to 0.1875
- delta_gate: bfloat16 [16, 7168, 128], P('exp', None, 'base'), may hold values from -0.0625 to 0.0625
- delta_up: bfloat16 [16, 7168, 128], P('exp', None, 'base'), may hold values from -0.0625 to 0.0625
- delta_down: bfloat16 [16, 128, 7168], P('exp', None, 'base'), may hold values from -0.5 to 0.5
- base_gate: bfloat16 [7168, 1024], P(None, 'base'), may hold values from -0.0625 to 0.0625
- base_up: bfloat16 [7168, 1024], P(None, 'base'), may hold values from -0.0625 to 0.0625
- base_down: bfloat16 [1024, 7168], P('base'), may hold values from -0.1875 to 0.1875
Outputs:
- errors: float32 [512], P(('grp', 'exp')), parts along dimension 0
There are 2 independent parts, one for each index of `grp`. A program takes and returns all parts, laid end to end along the dimension named above; an argument that names none is the same for every part. Nothing has to cross between parts.
Inputs may be any that keep to these rules, and one draw needn't show every extreme that they name: `expert_ids`: A token names 8 different experts; among the tokens of one index of exp no expert is named more than 48 times.
All inputs are finite; a program needn't handle non-finite values.
Results may differ from a plain program's by a relative error of at most 0.00064.
Values may be sent and summed in bfloat16 or wider, within the bound.
A program may use at most 256 MiB of HBM per device.

v0:
```python
import jax
import jax.numpy as jnp
from jax import lax
from jax.sharding import PartitionSpec as P

D = 7168


def swiglu(rows, gate_w, up_w):
    gate_pre = jnp.dot(rows, gate_w, preferred_element_type=jnp.float32)
    up_pre = jnp.dot(rows, up_w, preferred_element_type=jnp.float32)
    return (jax.nn.silu(gate_pre) * up_pre).astype(jnp.bfloat16)


def shards(
    tokens,
    expert_ids,
    gate_q,
    importance,
    dense_gate,
    dense_up,
    dense_down,
    delta_gate,
    delta_up,
    delta_down,
    base_gate,
    base_up,
    base_down,
):
    groups = lax.axis_size("exp")
    splits = lax.axis_size("base")
    tok_rows, local_width = tokens.shape
    top_k = expert_ids.shape[1]
    local_experts = dense_gate.shape[0]
    capacity = tok_rows * top_k * 3 // (2 * local_experts * groups)
    dense_width = dense_gate.shape[2]
    low_width = delta_gate.shape[2]
    all_rows = tok_rows * groups
    slots = capacity * groups
    routing = lax.all_gather(
        jnp.concatenate([expert_ids, gate_q], axis=1), "exp", axis=0, tiled=True
    )
    own_rows = lax.all_gather(tokens, "base", axis=1, tiled=True)
    rows = lax.all_gather(own_rows, "exp", axis=0, tiled=True)
    ids, gates = (routing[:, :top_k], routing[:, top_k:])
    first = lax.axis_index("exp") * local_experts
    mine = first + jnp.arange(local_experts, dtype=jnp.int32)
    hit = ids[:, None, :] == mine[None, :, None]
    weight = jnp.sum(jnp.where(hit, gates[:, None, :].astype(jnp.float32), 0.0), axis=2) / 65536.0
    named = jnp.any(hit, axis=2)
    order = jnp.arange(all_rows, dtype=jnp.int32)
    block = order // tok_rows
    before = (block[:, None] == block[None, :]) & (order[None, :] < order[:, None])
    position = jnp.dot(
        before.astype(jnp.bfloat16), named.astype(jnp.bfloat16), preferred_element_type=jnp.float32
    ).astype(jnp.int32)
    slot = jnp.where(named, block[:, None] * capacity + position, -1)
    pick = jnp.arange(slots, dtype=jnp.int32)[None, :, None] == slot.T[:, None, :]
    select = pick.astype(jnp.bfloat16)
    shared = swiglu(own_rows, base_gate, base_up)
    partial_value = jnp.dot(shared, base_down, preferred_element_type=jnp.float32)
    base_own = lax.psum_scatter(
        partial_value.astype(jnp.bfloat16), "base", scatter_dimension=1, tiled=True
    )
    base_all = lax.all_gather(base_own, "exp", axis=0, tiled=True)
    packed = []
    for j in range(local_experts):
        hidden = swiglu(rows, dense_gate[j], dense_up[j])
        low = swiglu(rows, delta_gate[j], delta_up[j])
        both = jnp.concatenate([hidden, low], axis=1)
        packed.append(
            jnp.dot(select[j], both, preferred_element_type=jnp.float32).astype(jnp.bfloat16)
        )
    sent = jnp.stack(packed)
    full = lax.all_gather(sent, "base", axis=0, tiled=False)
    total = jnp.zeros((all_rows,), jnp.float32)
    for j in range(local_experts):
        hid = jnp.concatenate([full[b, j, :, :dense_width] for b in range(splits)], axis=1)
        low = jnp.concatenate([full[b, j, :, dense_width:] for b in range(splits)], axis=1)
        residual = jnp.dot(hid, dense_down[j], preferred_element_type=jnp.float32) - jnp.dot(
            low, delta_down[j], preferred_element_type=jnp.float32
        )
        residual = residual.astype(jnp.bfloat16).astype(jnp.float32)
        base_rows = jnp.dot(select[j], base_all, preferred_element_type=jnp.float32)
        deviation = residual - base_rows
        squares = jnp.sum(importance * deviation * deviation, axis=1)
        back = jnp.sum(jnp.where(pick[j], squares[:, None], 0.0), axis=0)
        total = total + weight[:, j] * back
    total = lax.psum(total / D, ("exp", "base"))
    return lax.dynamic_slice_in_dim(total, lax.axis_index("exp") * tok_rows, tok_rows)


def solution(mesh):
    in_specs = (
        P(("grp", "exp"), "base"),
        P(("grp", "exp"), None),
        P(("grp", "exp"), None),
        P("base"),
        P("exp", None, "base"),
        P("exp", None, "base"),
        P("exp", None, "base"),
        P("exp", None, "base"),
        P("exp", None, "base"),
        P("exp", None, "base"),
        P(None, "base"),
        P(None, "base"),
        P("base", None),
    )
    out_specs = P(("grp", "exp"))
    return jax.shard_map(shards, mesh=mesh, in_specs=in_specs, out_specs=out_specs, check_vma=False)
```

profile of v0, /device:TPU:0, one launch (start us, length us, event | category | flops | bytes accessed | tf_op | source)
XLA Modules:
  0.0 204.3 jit_solution(16887898204992520157)
XLA Ops:
  7.4 23.4 %all_gather.19 = bf16[64,7168]{1,0:T(8,128)(2,1)} all-gather(bf16[64,1792]{1,0:T(8,128)(2,1)} %param.13), channel_id=1, replica_groups=mesh['grp'=2,'exp'=4,'base'=4] {'base'}, dimensions={1}, use_global_device_ids=true | all-gather | bytes 1146880 | tf_op jit(solution)/shard_map/all_gather | solution.py:43
  30.9 3.1 %fusion.206 = f32[64,256]{1,0:T(8,128)S(1)} fusion(bf16[64,7168]{1,0:T(8,128)(2,1)} %all_gather.19, bf16[7168,256]{1,0:T(8,128)(2,1)} %param.23), kind=kOutput, calls=%fused_computation.267 | convolution fusion | flops 234881024 | bytes 4653056 | tf_op jit(solution)/shard_map/dot_general | solution.py:10
  34.0 6.8 %convolution_convert_fusion = bf16[64,7168]{1,0:T(8,128)(2,1)} fusion(bf16[256,7168]{1,0:T(8,128)(2,1)} %param.25, bf16[64,7168]{1,0:T(8,128)(2,1)S(1)} %copy-done.1, bf16[7168,256]{1,0:T(8,128)(2,1)} %param.24, f32[64,256]{1,0:T(8,128)S(1)} %fusion.206), kind=kOutput, calls=%fused_computation | convolution fusion | flops 470319104 | bytes 9240576 | tf_op jit(solution)/shard_map/dot_general | solution.py:61
  40.9 5.5 %all-gather.1 = s32[4,64,16]{1,2,0:T(8,128)S(1)} all-gather(s32[1,64,16]{1,2,0:T(8,128)S(1)} %add_bitcast_fusion), channel_id=1, replica_groups=mesh['grp'=2,'exp'=4,'base'=4] {'exp'}, dimensions={0}, use_global_device_ids=true | all-gather | bytes 20480 | tf_op jit(solution)/shard_map/all_gather | solution.py:40
  47.0 15.2 %all-gather.5.cloned.1.call-done = bf16[256,7168]{1,0:T(8,128)(2,1)} async-done(((bf16[64,7168]{1,0:T(8,128)(2,1)}), bf16[256,7168]{1,0:T(8,128)(2,1)}) %all-gather.5.cloned.1.call-update) | async-done | bytes 3670032 | tf_op jit(solution)/shard_map/all_gather | solution.py:44
  62.2 3.4 %fusion.88 = f32[256,32]{0,1:T(8,128)S(1)} fusion(bf16[256,7168]{1,0:T(8,128)(2,1)} %all-gather.5.cloned.1.call-done, bf16[4,7168,32]{1,2,0:T(8,128)(2,1)S(1)} %copy-done.2), kind=kOutput, calls=%fused_computation.97 | convolution fusion | flops 117440512 | bytes 4161536 | tf_op jit(solution)/shard_map/dot_general | solution.py:10
  65.6 3.8 %fusion.10 = f32[256,256]{0,1:T(8,128)S(1)} fusion(bf16[256,7168]{1,0:T(8,128)(2,1)S(1)} %copy-done, bf16[4,7168,256]{2,1,0:T(8,128)(2,1)} %param.17), kind=kOutput, calls=%fused_computation.11 | convolution fusion | flops 939524096 | bytes 7602176 | tf_op jit(solution)/shard_map/dot_general | solution.py:10
  69.5 1.2 fusion.80
  70.7 3.9 %fusion.60 = bf16[256,256]{0,1:T(8,128)(2,1)S(1)} fusion(bf16[256,7168]{1,0:T(8,128)(2,1)S(1)} %copy-done, bf16[4,7168,256]{2,1,0:T(8,128)(2,1)} %param.18, f32[256,256]{0,1:T(8,128)S(1)} %fusion.10), kind=kOutput, calls=%fused_computation.69 | convolution fusion | flops 939917312 | bytes 7733248 | tf_op jit(solution)/shard_map/dot_general | solution.py:11
  74.8 1.2 fusion.91
  76.0 1.2 fusion.94
  77.2 1.2 fusion.97
  78.5 1.6 fusion.14
  80.1 1.6 fusion.18
  81.7 1.2 fusion.79
  82.9 1.2 fusion.78
  84.2 3.9 %fusion.63 = bf16[256,256]{0,1:T(8,128)(2,1)S(1)} fusion(bf16[256,7168]{1,0:T(8,128)(2,1)S(1)} %copy-done, bf16[4,7168,256]{2,1,0:T(8,128)(2,1)} %param.18, f32[256,256]{0,1:T(8,128)S(1)} %fusion.14), kind=kOutput, calls=%fused_computation.70 | convolution fusion | flops 939917312 | bytes 7733248 | tf_op jit(solution)/shard_map/dot_general | solution.py:11
  88.1 3.7 %fusion.66 = bf16[256,256]{0,1:T(8,128)(2,1)S(1)} fusion(bf16[256,7168]{1,0:T(8,128)(2,1)S(1)} %copy-done, bf16[4,7168,256]{2,1,0:T(8,128)(2,1)} %param.18, f32[256,256]{0,1:T(8,128)S(1)} %fusion.18), kind=kOutput, calls=%fused_computation.71 | convolution fusion | flops 939917312 | bytes 7733248 | tf_op jit(solution)/shard_map/dot_general | solution.py:11
  92.3 1.2 fusion.77
  93.5 1.6 fusion.22
  95.1 3.7 %fusion.69 = bf16[256,256]{0,1:T(8,128)(2,1)S(1)} fusion(bf16[256,7168]{1,0:T(8,128)(2,1)S(1)} %copy-done, bf16[4,7168,256]{2,1,0:T(8,128)(2,1)} %param.18, f32[256,256]{0,1:T(8,128)S(1)} %fusion.22), kind=kOutput, calls=%fused_computation.72 | convolution fusion | flops 939917312 | bytes 7733248 | tf_op jit(solution)/shard_map/dot_general | solution.py:11
  99.1 0.9 pad_maximum_fusion
  100.2 9.8 %all_gather.23 = bf16[256,1792]{1,0:T(8,128)(2,1)S(1)} all-gather(bf16[64,1792]{1,0:T(8,128)(2,1)} %reduce-scatter.2.cloned.1.call-done), channel_id=1, replica_groups=mesh['grp'=2,'exp'=4,'base'=4] {'exp'}, dimensions={0}, use_global_device_ids=true | all-gather | bytes 1146880 | tf_op jit(solution)/shard_map/all_gather | solution.py:65
  110.0 40.2 %all-gather.7.cloned.1.call-done = bf16[16,192,288]{2,1,0:T(8,128)(2,1)} async-done(((bf16[4,192,288]{2,1,0:T(8,128)(2,1)}), bf16[16,192,288]{2,1,0:T(8,128)(2,1)}) %all-gather.7.cloned.1.call-update) | async-done | bytes 1769488 | tf_op jit(solution)/shard_map/all_gather | solution.py:75
  150.2 1.2 slice_bitcast_fusion.39
  151.4 1.7 slice_bitcast_fusion.23
  153.1 3.1 %fusion.4 = f32[192,1792]{1,0:T(8,128)S(1)} fusion(bf16[4,1024,1792]{2,1,0:T(8,128)(2,1)} %param.19, bf16[192,256]{1,0:T(8,128)(2,1)S(1)} %get-tuple-element.34, bf16[192,256]{1,0:T(8,128)(2,1)S(1)} %get-tuple-element.35, bf16[192,256]{1,0:T(8,128)(2,1)S(1)} %get-tuple-element.36, bf16[192,256]{1,0:T(8,128)(2,1)S(1)} %get-tuple-element.25), kind=kOutput, calls=%fused_computation.5 | convolution fusion | flops 706215936 | bytes 5439488 | tf_op jit(solution)/shard_map/dot_general | solution.py:80
  157.1 3.1 %fusion = f32[192,1792]{1,0:T(8,128)S(1)} fusion(bf16[4,1024,1792]{2,1,0:T(8,128)(2,1)} %param.19, bf16[192,256]{1,0:T(8,128)(2,1)S(1)} %get-tuple-element.26, bf16[192,256]{1,0:T(8,128)(2,1)S(1)} %get-tuple-element.27, bf16[192,256]{1,0:T(8,128)(2,1)S(1)} %get-tuple-element.28, bf16[192,256]{1,0:T(8,128)(2,1)S(1)} %get-tuple-element.29), kind=kOutput, calls=%fused_computation.1 | convolution fusion | flops 706215936 | bytes 5439488 | tf_op jit(solution)/shard_map/dot_general | solution.py:80
  161.2 0.9 fusion.2
  163.0 0.9 fusion.6
  165.0 31.3 %psum.7 = f32[256]{0:T(256)S(1)} all-reduce(f32[256]{0:T(256)S(1)} %add_multiply_fusion), channel_id=1, replica_groups=mesh['grp'=2,'exp'=4,'base'=4] {'exp','base'}, use_global_device_ids=true, to_apply=%region_11.12 | all-reduce | flops 256 | bytes 2048 | tf_op jit(solution)/shard_map/psum | solution.py:89
  196.3 0.6 dynamic_slice.3
  (67 shorter events, 5.6 us)
Async XLA Ops:
  7.4 54.8 %all-gather.5.cloned.1.call-start = ((), (), s32[]{:S(2)}) async-start(), calls=%async_computation.1 | async-start | bytes 4587520 | tf_op jit(solution)/shard_map/all_gather | solution.py:44
  30.8 3.2 %copy-start.1 = (bf16[64,7168]{1,0:T(8,128)(2,1)S(1)}, bf16[64,7168]{1,0:T(8,128)(2,1)}, u32[]{:S(2)}) copy-start(bf16[64,7168]{1,0:T(8,128)(2,1)} %all_gather.19) | copy-start | bytes 2752516
  30.8 69.4 %reduce-scatter.2.cloned.1.call-start = ((), (), s32[]{:S(2)}) async-start(), calls=%async_computation.2 | async-start | bytes 1146880 | tf_op jit(solution)/shard_map/reduce_scatter | solution.py:62
  34.0 6.9 %copy-start.6 = (s32[64,8]{0,1:T(8,128)S(1)}, s32[64,8]{0,1:T(8,128)}, u32[]{:S(2)}) copy-start(s32[64,8]{0,1:T(8,128)} %param.15) | copy-start | bytes 6148
  34.0 6.9 %copy-start.7 = (s32[64,8]{0,1:T(8,128)S(1)}, s32[64,8]{0,1:T(8,128)}, u32[]{:S(2)}) copy-start(s32[64,8]{0,1:T(8,128)} %param.14) | copy-start | bytes 6148
  34.0 28.2 %copy-start.2 = (bf16[4,7168,32]{1,2,0:T(8,128)(2,1)S(1)}, bf16[4,7168,32]{1,2,0:T(8,128)(2,1)}, u32[]{:S(2)}) copy-start(bf16[4,7168,32]{1,2,0:T(8,128)(2,1)} %param.20) | copy-start | bytes 5505028
  40.8 109.4 %all-gather.7.cloned.1.call-start = ((), (), s32[]{:S(2)}) async-start(), calls=%async_computation.3 | async-start | bytes 2949120 | tf_op jit(solution)/shard_map/all_gather | solution.py:75
  62.2 3.4 %copy-start = (bf16[256,7168]{1,0:T(8,128)(2,1)S(1)}, bf16[256,7168]{1,0:T(8,128)(2,1)}, u32[]{:S(2)}) copy-start(bf16[256,7168]{1,0:T(8,128)(2,1)} %all-gather.5.cloned.1.call-done) | copy-start | bytes 11010052
  65.6 3.8 %copy-start.3 = (bf16[4,7168,32]{1,2,0:T(8,128)(2,1)S(1)}, bf16[4,7168,32]{1,2,0:T(8,128)(2,1)}, u32[]{:S(2)}) copy-start(bf16[4,7168,32]{1,2,0:T(8,128)(2,1)} %param.21) | copy-start | bytes 5505028
  69.5 9.0 %slice-start = ((s8[14680064]{0:T(1024)(128)(4,1)}), s8[4194304]{0:T(1024)(128)(4,1)S(1)}, s32[]{:S(2)}) async-start(s8[14680064]{0:T(1024)(128)(4,1)} %bitcast.227), calls=%async_computation.4 | async-start | bytes 8388608
  70.7 7.8 %slice-start.1 = ((s8[14680064]{0:T(1024)(128)(4,1)}), s8[4194304]{0:T(1024)(128)(4,1)S(1)}, s32[]{:S(2)}) async-start(s8[14680064]{0:T(1024)(128)(4,1)} %bitcast.227), calls=%async_computation.5 | async-start | bytes 8388608
  70.7 7.8 %slice-start.2 = ((s8[14680064]{0:T(1024)(128)(4,1)}), s8[4194304]{0:T(1024)(128)(4,1)S(1)}, s32[]{:S(2)}) async-start(s8[14680064]{0:T(1024)(128)(4,1)} %bitcast.227), calls=%async_computation.6 | async-start | bytes 8388608
  76.0 2.5 %slice-start.3 = ((s8[14680064]{0:T(1024)(128)(4,1)}), s8[2097152]{0:T(1024)(128)(4,1)S(1)}, s32[]{:S(2)}) async-start(s8[14680064]{0:T(1024)(128)(4,1)} %bitcast.227), calls=%async_computation.7 | async-start | bytes 4194304
  151.4 9.8 %slice-start.4 = ((s8[14680064]{0:T(1024)(128)(4,1)}), s8[2097152]{0:T(1024)(128)(4,1)S(1)}, s32[]{:S(2)}) async-start(s8[14680064]{0:T(1024)(128)(4,1)} %bitcast.229), calls=%async_computation.8 | async-start | bytes 4194304
  153.1 3.1 %copy-start.4 = (bf16[4,128,1792]{2,1,0:T(8,128)(2,1)S(1)}, bf16[4,128,1792]{2,1,0:T(8,128)(2,1)}, u32[]{:S(2)}) copy-start(bf16[4,128,1792]{2,1,0:T(8,128)(2,1)} %param.22) | copy-start | bytes 5505028
  153.1 3.5 %copy-start.5 = (f32[1792]{0:T(1024)S(1)}, f32[1792]{0:T(1024)}, u32[]{:S(2)}) copy-start(f32[1792]{0:T(1024)} %param.16) | copy-start | bytes 21508
  153.1 8.0 %slice-start.5 = ((s8[14680064]{0:T(1024)(128)(4,1)}), s8[4194304]{0:T(1024)(128)(4,1)S(1)}, s32[]{:S(2)}) async-start(s8[14680064]{0:T(1024)(128)(4,1)} %bitcast.229), calls=%async_computation.9 | async-start | bytes 8388608
  156.6 4.5 %slice-start.6 = ((s8[14680064]{0:T(1024)(128)(4,1)}), s8[4194304]{0:T(1024)(128)(4,1)S(1)}, s32[]{:S(2)}) async-start(s8[14680064]{0:T(1024)(128)(4,1)} %bitcast.229), calls=%async_computation.10 | async-start | bytes 8388608
  157.1 4.1 %slice-start.7 = ((s8[14680064]{0:T(1024)(128)(4,1)}), s8[4194304]{0:T(1024)(128)(4,1)S(1)}, s32[]{:S(2)}) async-start(s8[14680064]{0:T(1024)(128)(4,1)} %bitcast.229), calls=%async_computation.11 | async-start | bytes 8388608
Sparse Core Ops, SparseCore 0:
  30.9 31.2 all-gather.4
Sparse Core Ops, SparseCore 1:
  40.9 24.4 reduce-scatter.1
  100.1 50.0 all-gather.6
where the time goes:
time: 205 us; the launch traced here: 204 us
  blocking collectives  70 us (34%)
  matrix products  58.1 us (28%)
  waiting for transfers between devices  55.4 us (27%)
  between operations  15.3 us (7%)
  local copies, waits for them, and re-layouts  3.8 us (2%)
    all_gather x1, waiting for transfers between devices, shards(): full = lax.all_gather(sent, 'base', axis=0, tiled=False)  40.2 us
    psum x1, blocking collectives, shards(): total = lax.psum(total / D, ('exp', 'base'))  31.3 us
    all_gather x1, blocking collectives, shards(): own_rows = lax.all_gather(tokens, 'base', axis=1, tiled=True)  23.4 us
    dot_general x8, matrix products, swiglu(): up_pre = jnp.dot(rows, up_w, preferred_element_type=jnp.float32)  20.1 us
    dot_general x9, matrix products, swiglu(): gate_pre = jnp.dot(rows, gate_w, preferred_element_type=jnp.float32)  18.7 us
    all_gather x1, waiting for transfers between devices, shards(): rows = lax.all_gather(own_rows, 'exp', axis=0, tiled=True)  15.2 us
    all_gather x1, blocking collectives, shards(): base_all = lax.all_gather(base_own, 'exp', axis=0, tiled=True)  9.8 us
    dot_general x4, matrix products, shards(): jnp.dot(hid, dense_down[j], preferred_element_type=jnp.float32)  7.97 us
  transfers between devices with their start and end apart: 3, of which 2 were waited for; matrix products, arithmetic and copies ran while one was open for 24% of the time, Pallas kernels for 0%

commit v1 on v0

--- a/solution.py
+++ b/solution.py
@@ -2,6 +2,7 @@
 import jax.numpy as jnp
 from jax import lax
 from jax.sharding import PartitionSpec as P
+from jax.lax import psum
 
 D = 7168
 
@@ -86,7 +87,9 @@
         squares = jnp.sum(importance * deviation * deviation, axis=1)
         back = jnp.sum(jnp.where(pick[j], squares[:, None], 0.0), axis=0)
         total = total + weight[:, j] * back
-    total = lax.psum(total / D, ("exp", "base"))
+    total = total / D
+    for ii in ("base", "exp"):
+        total = psum(total, axis_name=ii)
     return lax.dynamic_slice_in_dim(total, lax.axis_index("exp") * tok_rows, tok_rows)
 
 

time: 205 us -> 189 us (0.922)
  blocking collectives: 70 us -> 54 us
    psum x1 -> x2, blocking collectives: 31.3 us -> 15.2 us  [shards(): total = psum(total, axis_name=ii)]
  transfers between devices with their start and end apart: 3 -> 3, of which waited for: 2 -> 2; matrix products, arithmetic and copies ran while one was open for 24% -> 26% of each run, Pallas kernels for 0% -> 0%
where the time goes in v1:
time: 189 us; the launch traced here: 188 us
  matrix products  58.2 us (31%)
  waiting for transfers between devices  55.3 us (29%)
  blocking collectives  54 us (29%)
  between operations  15.3 us (8%)
  local copies, waits for them, and re-layouts  3.79 us (2%)
    all_gather x1, waiting for transfers between devices, shards(): full = lax.all_gather(sent, 'base', axis=0, tiled=False)  40.2 us
    all_gather x1, blocking collectives, shards(): own_rows = lax.all_gather(tokens, 'base', axis=1, tiled=True)  23.4 us
    dot_general x8, matrix products, swiglu(): up_pre = jnp.dot(rows, up_w, preferred_element_type=jnp.float32)  20.1 us
    dot_general x9, matrix products, swiglu(): gate_pre = jnp.dot(rows, gate_w, preferred_element_type=jnp.float32)  18.7 us
    psum x2, blocking collectives, shards(): total = psum(total, axis_name=ii)  15.2 us
    all_gather x1, waiting for transfers between devices, shards(): rows = lax.all_gather(own_rows, 'exp', axis=0, tiled=True)  15.1 us
    all_gather x1, blocking collectives, shards(): base_all = lax.all_gather(base_own, 'exp', axis=0, tiled=True)  9.8 us
    dot_general x4, matrix products, shards(): jnp.dot(hid, dense_down[j], preferred_element_type=jnp.float32)  7.98 us
  transfers between devices with their start and end apart: 3, of which 2 were waited for; matrix products, arithmetic and copies ran while one was open for 26% of the time, Pallas kernels for 0%

profile of v1, /device:TPU:0, one launch (start us, length us, event | category | flops | bytes accessed | tf_op | source)
XLA Modules:
  0.0 188.2 jit_solution(9238779988478849201)
XLA Ops:
  7.4 23.4 %all_gather.19 = bf16[64,7168]{1,0:T(8,128)(2,1)} all-gather(bf16[64,1792]{1,0:T(8,128)(2,1)} %param.13), channel_id=1, replica_groups=mesh['grp'=2,'exp'=4,'base'=4] {'base'}, dimensions={1}, use_global_device_ids=true | all-gather | bytes 1146880 | tf_op jit(solution)/shard_map/all_gather | solution.py:44
  30.9 3.1 %fusion.206 = f32[64,256]{1,0:T(8,128)S(1)} fusion(bf16[64,7168]{1,0:T(8,128)(2,1)} %all_gather.19, bf16[7168,256]{1,0:T(8,128)(2,1)} %param.23), kind=kOutput, calls=%fused_computation.267 | convolution fusion | flops 234881024 | bytes 4653056 | tf_op jit(solution)/shard_map/dot_general | solution.py:11
  34.0 6.8 %convolution_convert_fusion = bf16[64,7168]{1,0:T(8,128)(2,1)} fusion(bf16[256,7168]{1,0:T(8,128)(2,1)} %param.25, bf16[64,7168]{1,0:T(8,128)(2,1)S(1)} %copy-done.1, bf16[7168,256]{1,0:T(8,128)(2,1)} %param.24, f32[64,256]{1,0:T(8,128)S(1)} %fusion.206), kind=kOutput, calls=%fused_computation | convolution fusion | flops 470319104 | bytes 9240576 | tf_op jit(solution)/shard_map/dot_general | solution.py:62
  40.9 5.5 %all-gather.1 = s32[4,64,16]{1,2,0:T(8,128)S(1)} all-gather(s32[1,64,16]{1,2,0:T(8,128)S(1)} %add_bitcast_fusion), channel_id=1, replica_groups=mesh['grp'=2,'exp'=4,'base'=4] {'exp'}, dimensions={0}, use_global_device_ids=true | all-gather | bytes 20480 | tf_op jit(solution)/shard_map/all_gather | solution.py:41
  47.0 15.1 %all-gather.5.cloned.1.call-done = bf16[256,7168]{1,0:T(8,128)(2,1)} async-done(((bf16[64,7168]{1,0:T(8,128)(2,1)}), bf16[256,7168]{1,0:T(8,128)(2,1)}) %all-gather.5.cloned.1.call-update) | async-done | bytes 3670032 | tf_op jit(solution)/shard_map/all_gather | solution.py:45
  62.1 3.4 %fusion.88 = f32[256,32]{0,1:T(8,128)S(1)} fusion(bf16[256,7168]{1,0:T(8,128)(2,1)} %all-gather.5.cloned.1.call-done, bf16[4,7168,32]{1,2,0:T(8,128)(2,1)S(1)} %copy-done.2), kind=kOutput, calls=%fused_computation.97 | convolution fusion | flops 117440512 | bytes 4161536 | tf_op jit(solution)/shard_map/dot_general | solution.py:11
  65.6 3.8 %fusion.10 = f32[256,256]{0,1:T(8,128)S(1)} fusion(bf16[256,7168]{1,0:T(8,128)(2,1)S(1)} %copy-done, bf16[4,7168,256]{2,1,0:T(8,128)(2,1)} %param.17), kind=kOutput, calls=%fused_computation.11 | convolution fusion | flops 939524096 | bytes 7602176 | tf_op jit(solution)/shard_map/dot_general | solution.py:11
  69.4 1.2 fusion.80
  70.7 3.9 %fusion.60 = bf16[256,256]{0,1:T(8,128)(2,1)S(1)} fusion(bf16[256,7168]{1,0:T(8,128)(2,1)S(1)} %copy-done, bf16[4,7168,256]{2,1,0:T(8,128)(2,1)} %param.18, f32[256,256]{0,1:T(8,128)S(1)} %fusion.10), kind=kOutput, calls=%fused_computation.69 | convolution fusion | flops 939917312 | bytes 7733248 | tf_op jit(solution)/shard_map/dot_general | solution.py:12
  74.8 1.2 fusion.91
  76.0 1.2 fusion.94
  77.2 1.2 fusion.97
  78.5 1.6 fusion.14
  80.1 1.6 fusion.18
  81.7 1.2 fusion.79
  82.9 1.2 fusion.78
  84.1 3.9 %fusion.63 = bf16[256,256]{0,1:T(8,128)(2,1)S(1)} fusion(bf16[256,7168]{1,0:T(8,128)(2,1)S(1)} %copy-done, bf16[4,7168,256]{2,1,0:T(8,128)(2,1)} %param.18, f32[256,256]{0,1:T(8,128)S(1)} %fusion.14), kind=kOutput, calls=%fused_computation.70 | convolution fusion | flops 939917312 | bytes 7733248 | tf_op jit(solution)/shard_map/dot_general | solution.py:12
  88.1 3.7 %fusion.66 = bf16[256,256]{0,1:T(8,128)(2,1)S(1)} fusion(bf16[256,7168]{1,0:T(8,128)(2,1)S(1)} %copy-done, bf16[4,7168,256]{2,1,0:T(8,128)(2,1)} %param.18, f32[256,256]{0,1:T(8,128)S(1)} %fusion.18), kind=kOutput, calls=%fused_computation.71 | convolution fusion | flops 939917312 | bytes 7733248 | tf_op jit(solution)/shard_map/dot_general | solution.py:12
  92.2 1.2 fusion.77
  93.5 1.6 fusion.22
  95.1 3.7 %fusion.69 = bf16[256,256]{0,1:T(8,128)(2,1)S(1)} fusion(bf16[256,7168]{1,0:T(8,128)(2,1)S(1)} %copy-done, bf16[4,7168,256]{2,1,0:T(8,128)(2,1)} %param.18, f32[256,256]{0,1:T(8,128)S(1)} %fusion.22), kind=kOutput, calls=%fused_computation.72 | convolution fusion | flops 939917312 | bytes 7733248 | tf_op jit(solution)/shard_map/dot_general | solution.py:12
  99.0 1.0 pad_maximum_fusion
  100.2 9.8 %all_gather.23 = bf16[256,1792]{1,0:T(8,128)(2,1)S(1)} all-gather(bf16[64,1792]{1,0:T(8,128)(2,1)} %reduce-scatter.2.cloned.1.call-done), channel_id=1, replica_groups=mesh['grp'=2,'exp'=4,'base'=4] {'exp'}, dimensions={0}, use_global_device_ids=true | all-gather | bytes 1146880 | tf_op jit(solution)/shard_map/all_gather | solution.py:66
  110.0 40.2 %all-gather.7.cloned.1.call-done = bf16[16,192,288]{2,1,0:T(8,128)(2,1)} async-done(((bf16[4,192,288]{2,1,0:T(8,128)(2,1)}), bf16[16,192,288]{2,1,0:T(8,128)(2,1)}) %all-gather.7.cloned.1.call-update) | async-done | bytes 1769488 | tf_op jit(solution)/shard_map/all_gather | solution.py:76
  150.1 1.2 slice_bitcast_fusion.39
  151.3 1.7 slice_bitcast_fusion.23
  153.1 3.1 %fusion.4 = f32[192,1792]{1,0:T(8,128)S(1)} fusion(bf16[4,1024,1792]{2,1,0:T(8,128)(2,1)} %param.19, bf16[192,256]{1,0:T(8,128)(2,1)S(1)} %get-tuple-element.34, bf16[192,256]{1,0:T(8,128)(2,1)S(1)} %get-tuple-element.35, bf16[192,256]{1,0:T(8,128)(2,1)S(1)} %get-tuple-element.36, bf16[192,256]{1,0:T(8,128)(2,1)S(1)} %get-tuple-element.25), kind=kOutput, calls=%fused_computation.5 | convolution fusion | flops 706215936 | bytes 5439488 | tf_op jit(solution)/shard_map/dot_general | solution.py:81
  157.1 3.1 %fusion = f32[192,1792]{1,0:T(8,128)S(1)} fusion(bf16[4,1024,1792]{2,1,0:T(8,128)(2,1)} %param.19, bf16[192,256]{1,0:T(8,128)(2,1)S(1)} %get-tuple-element.26, bf16[192,256]{1,0:T(8,128)(2,1)S(1)} %get-tuple-element.27, bf16[192,256]{1,0:T(8,128)(2,1)S(1)} %get-tuple-element.28, bf16[192,256]{1,0:T(8,128)(2,1)S(1)} %get-tuple-element.29), kind=kOutput, calls=%fused_computation.1 | convolution fusion | flops 706215936 | bytes 5439488 | tf_op jit(solution)/shard_map/dot_general | solution.py:81
  161.2 0.9 fusion.2
  163.0 0.9 fusion.6
  164.9 9.6 %psum.14 = f32[256]{0:T(256)S(1)} all-reduce(f32[256]{0:T(256)S(1)} %add_multiply_fusion), channel_id=1, replica_groups=mesh['grp'=2,'exp'=4,'base'=4] {'base'}, use_global_device_ids=true, to_apply=%region_11.12 | all-reduce | flops 256 | bytes 2048 | tf_op jit(solution)/shard_map/psum | solution.py:92
  174.5 5.6 %psum.15 = f32[256]{0:T(256)S(1)} all-reduce(f32[256]{0:T(256)S(1)} %psum.14), channel_id=1, replica_groups=mesh['grp'=2,'exp'=4,'base'=4] {'exp'}, use_global_device_ids=true, to_apply=%region_12.13 | all-reduce | flops 256 | bytes 2048 | tf_op jit(solution)/shard_map/psum | solution.py:92
  (68 shorter events, 6.2 us)
Async XLA Ops:
  7.4 54.8 %all-gather.5.cloned.1.call-start = ((), (), s32[]{:S(2)}) async-start(), calls=%async_computation.1 | async-start | bytes 4587520 | tf_op jit(solution)/shard_map/all_gather | solution.py:45
  30.8 3.2 %copy-start.1 = (bf16[64,7168]{1,0:T(8,128)(2,1)S(1)}, bf16[64,7168]{1,0:T(8,128)(2,1)}, u32[]{:S(2)}) copy-start(bf16[64,7168]{1,0:T(8,128)(2,1)} %all_gather.19) | copy-start | bytes 2752516
  30.8 69.3 %reduce-scatter.2.cloned.1.call-start = ((), (), s32[]{:S(2)}) async-start(), calls=%async_computation.2 | async-start | bytes 1146880 | tf_op jit(solution)/shard_map/reduce_scatter | solution.py:63
  34.0 6.9 %copy-start.6 = (s32[64,8]{0,1:T(8,128)S(1)}, s32[64,8]{0,1:T(8,128)}, u32[]{:S(2)}) copy-start(s32[64,8]{0,1:T(8,128)} %param.15) | copy-start | bytes 6148
  34.0 6.9 %copy-start.7 = (s32[64,8]{0,1:T(8,128)S(1)}, s32[64,8]{0,1:T(8,128)}, u32[]{:S(2)}) copy-start(s32[64,8]{0,1:T(8,128)} %param.14) | copy-start | bytes 6148
  34.0 28.1 %copy-start.2 = (bf16[4,7168,32]{1,2,0:T(8,128)(2,1)S(1)}, bf16[4,7168,32]{1,2,0:T(8,128)(2,1)}, u32[]{:S(2)}) copy-start(bf16[4,7168,32]{1,2,0:T(8,128)(2,1)} %param.20) | copy-start | bytes 5505028
  40.8 109.3 %all-gather.7.cloned.1.call-start = ((), (), s32[]{:S(2)}) async-start(), calls=%async_computation.3 | async-start | bytes 2949120 | tf_op jit(solution)/shard_map/all_gather | solution.py:76
  62.1 3.4 %copy-start = (bf16[256,7168]{1,0:T(8,128)(2,1)S(1)}, bf16[256,7168]{1,0:T(8,128)(2,1)}, u32[]{:S(2)}) copy-start(bf16[256,7168]{1,0:T(8,128)(2,1)} %all-gather.5.cloned.1.call-done) | copy-start | bytes 11010052
  65.6 3.8 %copy-start.3 = (bf16[4,7168,32]{1,2,0:T(8,128)(2,1)S(1)}, bf16[4,7168,32]{1,2,0:T(8,128)(2,1)}, u32[]{:S(2)}) copy-start(bf16[4,7168,32]{1,2,0:T(8,128)(2,1)} %param.21) | copy-start | bytes 5505028
  69.4 9.0 %slice-start = ((s8[14680064]{0:T(1024)(128)(4,1)}), s8[4194304]{0:T(1024)(128)(4,1)S(1)}, s32[]{:S(2)}) async-start(s8[14680064]{0:T(1024)(128)(4,1)} %bitcast.227), calls=%async_computation.4 | async-start | bytes 8388608
  70.6 7.8 %slice-start.1 = ((s8[14680064]{0:T(1024)(128)(4,1)}), s8[4194304]{0:T(1024)(128)(4,1)S(1)}, s32[]{:S(2)}) async-start(s8[14680064]{0:T(1024)(128)(4,1)} %bitcast.227), calls=%async_computation.5 | async-start | bytes 8388608
  70.7 7.8 %slice-start.2 = ((s8[14680064]{0:T(1024)(128)(4,1)}), s8[4194304]{0:T(1024)(128)(4,1)S(1)}, s32[]{:S(2)}) async-start(s8[14680064]{0:T(1024)(128)(4,1)} %bitcast.227), calls=%async_computation.6 | async-start | bytes 8388608
  76.0 2.5 %slice-start.3 = ((s8[14680064]{0:T(1024)(128)(4,1)}), s8[2097152]{0:T(1024)(128)(4,1)S(1)}, s32[]{:S(2)}) async-start(s8[14680064]{0:T(1024)(128)(4,1)} %bitcast.227), calls=%async_computation.7 | async-start | bytes 4194304
  151.3 9.8 %slice-start.4 = ((s8[14680064]{0:T(1024)(128)(4,1)}), s8[2097152]{0:T(1024)(128)(4,1)S(1)}, s32[]{:S(2)}) async-start(s8[14680064]{0:T(1024)(128)(4,1)} %bitcast.229), calls=%async_computation.8 | async-start | bytes 4194304
  153.1 3.1 %copy-start.4 = (bf16[4,128,1792]{2,1,0:T(8,128)(2,1)S(1)}, bf16[4,128,1792]{2,1,0:T(8,128)(2,1)}, u32[]{:S(2)}) copy-start(bf16[4,128,1792]{2,1,0:T(8,128)(2,1)} %param.22) | copy-start | bytes 5505028
  153.1 3.5 %copy-start.5 = (f32[1792]{0:T(1024)S(1)}, f32[1792]{0:T(1024)}, u32[]{:S(2)}) copy-start(f32[1792]{0:T(1024)} %param.16) | copy-start | bytes 21508
  153.1 8.0 %slice-start.5 = ((s8[14680064]{0:T(1024)(128)(4,1)}), s8[4194304]{0:T(1024)(128)(4,1)S(1)}, s32[]{:S(2)}) async-start(s8[14680064]{0:T(1024)(128)(4,1)} %bitcast.229), calls=%async_computation.9 | async-start | bytes 8388608
  156.6 4.5 %slice-start.6 = ((s8[14680064]{0:T(1024)(128)(4,1)}), s8[4194304]{0:T(1024)(128)(4,1)S(1)}, s32[]{:S(2)}) async-start(s8[14680064]{0:T(1024)(128)(4,1)} %bitcast.229), calls=%async_computation.10 | async-start | bytes 8388608
  157.1 4.1 %slice-start.7 = ((s8[14680064]{0:T(1024)(128)(4,1)}), s8[4194304]{0:T(1024)(128)(4,1)S(1)}, s32[]{:S(2)}) async-start(s8[14680064]{0:T(1024)(128)(4,1)} %bitcast.229), calls=%async_computation.11 | async-start | bytes 8388608
Sparse Core Ops, SparseCore 0:
  30.9 31.1 all-gather.4
Sparse Core Ops, SparseCore 1:
  40.9 24.3 reduce-scatter.1
  100.1 50.0 all-gather.6
